TPU v7x, 32 devices: a whole 2x2x4 slice. The times are simulated.
32 devices in a mesh: inst: 8 (over y, x, core), space: 4 (over z).
Axes of the slice: x: 2, y: 2, z: 4, core: 2. Of those that a mesh axis runs over, the one named last changes fastest.
Arguments:
- flow_state: float32 [8, 6, 256, 128], P('inst', None, 'space'), may hold values from -6 to 6
- forcing: float32 [8, 6, 256, 128], P('inst', None, 'space'), may hold values from -6 to 6
- pivot_table: float32 [8, 6, 6, 128], replicated, may hold values from -0.21 to 1, as said below
- block_offset: int32 [256], P('space'), may hold values from 0 to 7
- line_perm: int32 [128], replicated, may hold values from 0 to 127, each once
- axial_jac: float32 [6, 6], replicated, may hold values from -2.5 to 2.5
- radial_jac: float32 [6, 6], replicated, may hold values from -2.5 to 2.5
- lower_block: float32 [6, 6], replicated, may hold values from -0.035 to 0.97, as said below
- upper_block: float32 [6, 6], replicated, may hold values from -0.035 to 0.97, as said below
Outputs:
- residual: float32 [8, 6, 256, 128], P('inst', None, 'space')
- correction: float32 [8, 6, 256, 128], P('inst', None, 'space')
Inputs may be any that keep to these rules, and one draw needn't show every extreme that they name: `pivot_table`: diagonal entries lie in 0.6 to 1. `lower_block`: diagonal entries lie in 0.3 to 0.97, the others in -0.035 to 0.035. `upper_block`: diagonal entries lie in 0.3 to 0.97, the others in -0.035 to 0.035.
All inputs are finite; a program needn't handle non-finite values.
Results may differ from a plain program's by a relative error of at most 0.0001.
Values sent between devices are 32-bit elements; how exact they have to be, the bound alone decides.
A program may use at most 64 MiB of HBM per device.

v0:
```python
import functools

import jax
import jax.numpy as jnp
import numpy as np
from jax import lax
from jax.experimental import pallas as pl
from jax.experimental.pallas import tpu as pltpu
from jax.sharding import PartitionSpec as P

frequency = 0.5
viscosity = 0.01
damping = 0.25

f32 = jnp.float32
MESH = pl.DeviceIdType.MESH
NV = 6
NP = NV // 2
SEG = 8


def spectral_matrix(count):
    index = np.arange(count)
    distance = index[:, None] - index[None, :]
    parity = 1.0 - 2.0 * (distance % 2)
    angle = np.pi * distance / count
    diagonal = distance == 0
    sine = np.where(diagonal, 1.0, np.sin(angle))
    first = np.where(diagonal, 0.0, 0.5 * parity * np.cos(angle) / sine)
    second = np.where(diagonal, -(count * count + 2) / 12.0, -0.5 * parity / (sine * sine))
    return (frequency * first - viscosity * second).astype(np.float32)


def select_columns(x, onehot):
    high = x.astype(jnp.bfloat16)
    rest = x - high.astype(f32)
    middle = rest.astype(jnp.bfloat16)
    low = (rest - middle.astype(f32)).astype(jnp.bfloat16)
    out = jnp.dot(high, onehot, preferred_element_type=f32)
    out = out + jnp.dot(middle, onehot, preferred_element_type=f32)
    return out + jnp.dot(low, onehot, preferred_element_type=f32)


def kernel(
    count,
    spaces,
    state,
    forcing,
    pivot,
    offset,
    perm,
    ajac,
    rjac,
    lower,
    upper,
    res_out,
    cor_out,
    line,
    base,
    send1,
    recv1,
    send2,
    recv2,
    halo_out,
    halo_in,
    tab,
    coef,
    trans,
    rhs,
    sweep0,
    sweep1,
    ssem1,
    rsem1,
    ssem2,
    rsem2,
    hssem,
    hrsem,
):
    stations, radial = state.shape[1], state.shape[2]
    per = stations // count
    steps = radial // SEG
    spectral = spectral_matrix(count)
    me = lax.axis_index("inst")
    here = lax.axis_index("space")
    up = lax.rem(here + 1, spaces)
    down = lax.rem(here + spaces - 1, spaces)

    barrier = pltpu.get_barrier_semaphore()
    for d in range(1, count):
        pl.semaphore_signal(
            barrier, inc=1, device_id={"inst": lax.rem(me + d, count)}, device_id_type=MESH
        )
    for other in (up, down):
        pl.semaphore_signal(barrier, inc=1, device_id={"space": other}, device_id_type=MESH)

    rows = lax.broadcasted_iota(jnp.int32, (radial, radial), 0)
    order = (rows == perm[...]).astype(f32).astype(jnp.bfloat16)
    flat = select_columns(state[...].reshape(NV * stations, radial), order)
    for v in range(NV):
        block = flat[v * stations : (v + 1) * stations]
        line[v, 8 : 8 + stations, :] = block
        halo_out[0, v : v + 1, :] = block[0:1]
        halo_out[1, v : v + 1, :] = block[stations - 1 : stations]
        for e in range(count):
            send1[e, v * per : (v + 1) * per, :] = block[e * per : (e + 1) * per]

    pl.semaphore_wait(barrier, count + 1)

    def exchange(source, target, ssem, rsem):
        copies = []
        for d in range(count - 1, 0, -1):
            other = lax.rem(me + d, count)
            copies.append(
                pltpu.make_async_remote_copy(
                    src_ref=source.at[other],
                    dst_ref=target.at[me],
                    send_sem=ssem.at[d - 1],
                    recv_sem=rsem.at[d - 1],
                    device_id={"inst": other},
                    device_id_type=MESH,
                )
            )
        return copies

    first = exchange(send1, recv1, ssem1, rsem1)
    for copy in first:
        copy.start()
    halos = []
    for side, other in ((0, down), (1, up)):
        halos.append(
            pltpu.make_async_remote_copy(
                src_ref=halo_out.at[side],
                dst_ref=halo_in.at[side],
                send_sem=hssem.at[side],
                recv_sem=hrsem.at[side],
                device_id={"space": other},
                device_id_type=MESH,
            )
        )
    for copy in halos:
        copy.start()
    recv1[me] = send1[me]

    def place(kind, v, w):
        p, h = v // 2, v % 2
        q, crossed = w // 2, (v % 2) ^ (w % 2)
        return ((((kind * NP + p) * NP + q) * 2 + crossed) * 2 + h) * 8

    tab[...] = jnp.zeros_like(tab)
    for v in range(NV):
        for k in range(8):
            block = pivot[k, v]
            for w in range(NV):
                at = place(0, v, w) + k
                tab[at : at + 1, :] = block[w : w + 1, :]
    for kind, matrix in ((1, lower), (2, upper)):
        for v in range(NV):
            parts = [tab[place(0, v, u) : place(0, v, u) + 8, :] for u in range(NV)]
            for w in range(NV):
                total = parts[0] * matrix[0, w]
                for u in range(1, NV):
                    total = total + parts[u] * matrix[u, w]
                at = place(kind, v, w)
                tab[at : at + 8, :] = -total

    lane = lax.broadcasted_iota(jnp.int32, (128, 256), 1)
    row = lax.broadcasted_iota(jnp.int32, (128, 256), 0)
    wanted = offset[...]
    for g in range(4):
        hit = (row - 32 * g == (lane // 64) * 8 + wanted)
        rhs[g] = hit.astype(f32).astype(jnp.bfloat16)

    def expand(b, carry):
        block = tab[pl.ds(pl.multiple_of(b * 128, 128), 128), :].T
        for g in range(4):
            both = select_columns(block, rhs[g])
            coef[b * 8 + 2 * g] = both[:, :128]
            coef[b * 8 + 2 * g + 1] = both[:, 128:]
        return carry

    lax.fori_loop(0, tab.shape[0] // 128, expand, 0)

    def at_step(t):
        return pl.ds(t, SEG, stride=steps)

    def crossed(pairs):
        return [pltpu.roll(x, 64, 1) for x in pairs]

    def apply(coefs, pairs, turned, start=None):
        out = []
        for p in range(NP):
            total = None if start is None else start[p]
            for q in range(NP):
                term = coefs[p][q][0] * pairs[q] + coefs[p][q][1] * turned[q]
                total = term if total is None else total + term
            out.append(total)
        return out

    def load_coefs(kind, t):
        return [
            [
                [coef[((kind * NP + p) * NP + q) * 2 + c, at_step(t), :] for c in range(2)]
                for q in range(NP)
            ]
            for p in range(NP)
        ]

    half = lax.broadcasted_iota(jnp.int32, (SEG, 128), 1) // 64
    unit = [
        [jnp.where(2 * q + half == u, 1.0, 0.0).astype(f32) for q in range(NP)] for u in range(NV)
    ]
    for kind in (0, 1):

        def transfer(i, columns):
            t = i if kind == 0 else steps - 1 - i
            coefs = load_coefs(kind + 1, t)
            new = []
            for u in range(NV):
                got = apply(coefs, columns[u], crossed(columns[u]))
                for p in range(NP):
                    trans[(kind * NV + u) * NP + p, at_step(t), :] = got[p]
                new.append(got)
            return new

        lax.fori_loop(0, steps, transfer, unit)

    order_forcing = select_columns(forcing[...].reshape(NV * stations, radial), order)
    for copy in halos:
        copy.wait_recv()
    for v in range(NV):
        line[v, 8 + stations : 9 + stations, :] = jnp.where(
            here == spaces - 1, 0.0, halo_in[0, v : v + 1, :]
        )
        line[v, 7:8, :] = jnp.where(here == 0, 0.0, halo_in[1, v : v + 1, :])

    spot = lax.broadcasted_iota(jnp.int32, (8, radial), 1)

    def local(i, carry):
        at = pl.multiple_of(i * 8, 8)
        axial, outward, mean = [], [], []
        for v in range(NV):
            window = line[v, pl.ds(at, 24), :]
            centre = window[8:16]
            ahead = window[9:17]
            behind = window[7:15]
            outer = jnp.where(spot == radial - 1, 0.0, pltpu.roll(centre, radial - 1, 1))
            inner = jnp.where(spot == 0, 0.0, pltpu.roll(centre, 1, 1))
            axial.append(0.5 * (ahead - behind))
            outward.append(0.5 * (outer - inner))
            mean.append(damping * (ahead + behind + outer + inner - 4.0 * centre))
        for v in range(NV):
            total = ajac[v, 0] * axial[0] + rjac[v, 0] * outward[0]
            for w in range(1, NV):
                total = total + (ajac[v, w] * axial[w] + rjac[v, w] * outward[w])
            base[v, pl.ds(at, 8), :] = total - mean[v]
        return carry

    lax.fori_loop(0, stations // 8, local, 0)
    for v in range(NV):
        base[v] = base[v] - order_forcing[v * stations : (v + 1) * stations]

    for copy in first:
        copy.wait_recv()
    for n in range(count):
        total = float(spectral[n, 0]) * recv1[0]
        for m in range(1, count):
            total = total + float(spectral[n, m]) * recv1[m]
        send2[n] = total
    second = exchange(send2, recv2, ssem2, rsem2)
    for copy in second:
        copy.start()
    recv2[me] = send2[me]
    for copy in second:
        copy.wait_recv()

    pairs = []
    for p in range(NP):
        blocks = []
        for v in (2 * p, 2 * p + 1):
            timed = jnp.concatenate(
                [recv2[e, v * per : (v + 1) * per, :] for e in range(count)], axis=0
            )
            residual = base[v] + timed
            res_out[v] = residual
            blocks.append(residual)
        sweep0[p] = jnp.concatenate(blocks, axis=0).T

    zeros = [jnp.zeros((SEG, 128), f32) for _ in range(NP)]
    segment = lax.broadcasted_iota(jnp.int32, (SEG, 128), 0)

    def spread(pairs):
        turned = crossed(pairs)
        out = []
        for q in range(NP):
            out.append(jnp.where(half == 0, pairs[q], turned[q]))
            out.append(jnp.where(half == 0, turned[q], pairs[q]))
        return out

    def add_transfer(kind, t, start, spreaded):
        out = []
        for p in range(NP):
            total = start[p]
            for u in range(NV):
                total = total + trans[(kind * NV + u) * NP + p, at_step(t), :] * spreaded[u]
            out.append(total)
        return out

    def carries(kind, last, ends):
        def turn(i, held):
            got = add_transfer(kind, last, ends, spread(held))
            shift, edge = (1, 0) if kind == 0 else (SEG - 1, SEG - 1)
            return [jnp.where(segment == edge, 0.0, pltpu.roll(x, shift, 0)) for x in got]

        return spread(lax.fori_loop(0, SEG - 1, turn, zeros))

    def forward(t, held):
        source = [sweep0[p, at_step(t), :] for p in range(NP)]
        start = apply(load_coefs(0, t), source, crossed(source))
        got = apply(load_coefs(1, t), held, crossed(held), start)
        for p in range(NP):
            sweep1[p, at_step(t), :] = got[p]
        return got

    ends = lax.fori_loop(0, steps, forward, zeros)
    entering = carries(0, steps - 1, ends)

    def backward(i, held):
        t = steps - 1 - i
        start = add_transfer(0, t, [sweep1[p, at_step(t), :] for p in range(NP)], entering)
        got = apply(load_coefs(2, t), held, crossed(held), start)
        for p in range(NP):
            sweep0[p, at_step(t), :] = got[p]
        return got

    ends = lax.fori_loop(0, steps, backward, zeros)
    leaving = carries(1, 0, ends)

    def finish(t, carry):
        got = add_transfer(1, t, [sweep0[p, at_step(t), :] for p in range(NP)], leaving)
        for p in range(NP):
            sweep1[p, at_step(t), :] = got[p]
        return carry

    lax.fori_loop(0, steps, finish, 0)
    for p in range(NP):
        block = sweep1[p].T
        cor_out[2 * p] = block[:stations]
        cor_out[2 * p + 1] = block[stations:]

    for copy in first + halos + second:
        copy.wait_send()


def shards(
    count,
    spaces,
    flow_state,
    forcing,
    pivot_table,
    block_offset,
    line_perm,
    axial_jac,
    radial_jac,
    lower_block,
    upper_block,
):
    _, variables, stations, radial = flow_state.shape
    per = stations // count
    block = jax.ShapeDtypeStruct((variables, stations, radial), f32)
    vmem = pl.BlockSpec(memory_space=pltpu.VMEM)
    smem = pl.BlockSpec(memory_space=pltpu.SMEM)
    dma = pltpu.SemaphoreType.DMA
    exchanged = pltpu.VMEM((count, variables * per, radial), f32)
    residual, correction = pl.pallas_call(
        functools.partial(kernel, count, spaces),
        out_shape=(block, block),
        in_specs=[vmem] * 5 + [smem] * 4,
        out_specs=(vmem, vmem),
        scratch_shapes=[
            pltpu.VMEM((variables, stations + 16, radial), f32),
            pltpu.VMEM((variables, stations, radial), f32),
            exchanged,
            exchanged,
            exchanged,
            exchanged,
            pltpu.VMEM((2, variables, radial), f32),
            pltpu.VMEM((2, variables, radial), f32),
            pltpu.VMEM((896, radial), f32),
            pltpu.VMEM((56, radial, 128), f32),
            pltpu.VMEM((36, radial, 128), f32),
            pltpu.VMEM((4, 128, 256), jnp.bfloat16),
            pltpu.VMEM((NP, radial, 128), f32),
            pltpu.VMEM((NP, radial, 128), f32),
            dma((count - 1,)),
            dma((count - 1,)),
            dma((count - 1,)),
            dma((count - 1,)),
            dma((2,)),
            dma((2,)),
        ],
        compiler_params=pltpu.CompilerParams(
            collective_id=0, has_side_effects=True, vmem_limit_bytes=40 * 1024 * 1024
        ),
    )(
        flow_state[0],
        forcing[0],
        pivot_table,
        jnp.tile(block_offset, 4).reshape(1, 4 * stations),
        line_perm.reshape(1, radial),
        axial_jac,
        radial_jac,
        lower_block,
        upper_block,
    )
    return residual[None], correction[None]


def solution(mesh):
    spec = P("inst", None, "space", None)
    return jax.shard_map(
        functools.partial(shards, mesh.shape["inst"], mesh.shape["space"]),
        mesh=mesh,
        in_specs=(spec, spec, P(), P("space"), P(), P(), P(), P(), P()),
        out_specs=(spec, spec),
        check_vma=False,
    )
```

profile of v0, /device:TPU:0, one launch (start us, length us, event | category | flops | bytes accessed | tf_op | source)
XLA Modules:
  0.0 29.6 jit_solution(9800905795489431841)
XLA Ops:
  0.6 0.0 copy-start
  0.6 0.7 %tile.2 = s32[4,64]{1,0:T(4,128)S(1)} broadcast(s32[64]{0:T(128)} %param.12), dimensions={1} | broadcast | bytes 1280 | tf_op jit(solution)/shard_map/tile | solution.py:408
  1.3 0.1 reshape_tile.3.offset
  1.4 0.0 copy-start.2
  1.4 0.0 copy-start.3
  1.4 0.0 copy-start.4
  1.4 0.0 copy-start.5
  1.4 0.0 copy-start.6
  1.4 1.0 %copy.11.pivot = f32[8,6,6,128]{3,2,1,0:T(8,128)S(1)} copy(f32[8,6,6,128]{3,0,2,1:T(8,128)} %param.11) | data formatting | bytes 294912 | tf_op args[2]
  2.5 0.0 copy-done
  2.5 0.0 copy-done.2
  2.5 0.0 copy-done.3
  2.5 0.0 copy-done.4
  2.5 0.0 copy-done.5
  2.5 0.0 copy-done.6
  2.5 0.0 copy-start.1
  2.5 0.9 %copy-done.1 = f32[1,6,64,128]{3,2,1,0:T(8,128)S(1)} copy-done((f32[1,6,64,128]{3,2,1,0:T(8,128)S(1)}, f32[1,6,64,128]{3,2,1,0:T(8,128)}, u32[]{:S(2)}) %copy-start.1) | copy-done | bytes 196632
  3.4 24.8 %shard_map.104 = (f32[6,64,128]{2,1,0:T(8,128)S(1)}, f32[6,64,128]{2,1,0:T(8,128)S(1)}) custom-call(f32[6,64,128]{2,1,0:T(8,128)S(1)} %bitcast.7, f32[6,64,128]{2,1,0:T(8,128)S(1)} %bitcast.8, f32[8,6,6,128]{3,2,1,0:T(8,128)S(1)} %copy.11.pivot, s32[1,256]{1,0:T(1,128)S(1)} %reshape_tile.3.offset, s32[1,128]{1,0:T(1,128)S(1)} %bitcast.9, ...), custom_call_target="tpu_custom_call" | custom-call | tf_op jit(solution)/shard_map/pallas_call | solution.py:374
  28.3 0.7 %copy.14 = f32[1,6,64,128]{3,2,1,0:T(8,128)} copy(f32[1,6,64,128]{3,2,1,0:T(8,128)S(1)} %bitcast.6) | data formatting | bytes 393216
  29.0 0.7 %copy.15 = f32[1,6,64,128]{3,2,1,0:T(8,128)} copy(f32[1,6,64,128]{3,2,1,0:T(8,128)S(1)} %bitcast.5) | data formatting | bytes 393216
Async XLA Ops:
  0.6 1.8 %copy-start = (f32[1,6,64,128]{3,2,1,0:T(8,128)S(1)}, f32[1,6,64,128]{3,2,1,0:T(8,128)}, u32[]{:S(2)}) copy-start(f32[1,6,64,128]{3,2,1,0:T(8,128)} %param.9) | copy-start | bytes 589828
  1.4 1.0 %copy-start.2 = (f32[6,6]{1,0:T(8,128)S(1)}, f32[6,6]{1,0:T(8,128)}, u32[]{:S(2)}) copy-start(f32[6,6]{1,0:T(8,128)} %ajac.1) | copy-start | bytes 436
  1.4 1.1 %copy-start.3 = (f32[6,6]{1,0:T(8,128)S(1)}, f32[6,6]{1,0:T(8,128)}, u32[]{:S(2)}) copy-start(f32[6,6]{1,0:T(8,128)} %rjac.1) | copy-start | bytes 436
  1.4 1.1 %copy-start.4 = (f32[6,6]{1,0:T(8,128)S(1)}, f32[6,6]{1,0:T(8,128)}, u32[]{:S(2)}) copy-start(f32[6,6]{1,0:T(8,128)} %lower.1) | copy-start | bytes 436
  1.4 1.1 %copy-start.5 = (f32[6,6]{1,0:T(8,128)S(1)}, f32[6,6]{1,0:T(8,128)}, u32[]{:S(2)}) copy-start(f32[6,6]{1,0:T(8,128)} %upper.1) | copy-start | bytes 436
  1.4 1.1 %copy-start.6 = (s32[128]{0:T(128)S(1)}, s32[128]{0:T(128)}, u32[]{:S(2)}) copy-start(s32[128]{0:T(128)} %param.13) | copy-start | bytes 1540
  2.5 0.9 %copy-start.1 = (f32[1,6,64,128]{3,2,1,0:T(8,128)S(1)}, f32[1,6,64,128]{3,2,1,0:T(8,128)}, u32[]{:S(2)}) copy-start(f32[1,6,64,128]{3,2,1,0:T(8,128)} %param.10) | copy-start | bytes 589828
where the time goes:
time: 29.8 us; the launch traced here: 29.6 us
  Pallas kernels  24.8 us (83%)
  local copies, waits for them, and re-layouts  4.09 us (14%)
  between operations  0.72 us (2%)
    pallas_call x1, Pallas kernels, shards(): pl.pallas_call(functools.partial(kernel, count, spaces), out_shape=(block...  24.8 us
    unnamed x17, local copies, waits for them, and re-layouts  3.31 us
    another operation x2, local copies, waits for them, and re-layouts, shards(): jnp.tile(block_offset, 4).reshape(1, 4 * stations)  0.78 us

commit v1 on v0

--- a/solution.py
+++ b/solution.py
@@ -44,6 +44,17 @@
 def kernel(
     count,
     spaces,
+    state_in,
+    forcing_in,
+    pivot_in,
+    offset_in,
+    perm_in,
+    ajac_in,
+    rjac_in,
+    lower_in,
+    upper_in,
+    res_out,
+    cor_out,
     state,
     forcing,
     pivot,
@@ -53,8 +64,7 @@
     rjac,
     lower,
     upper,
-    res_out,
-    cor_out,
+    insem,
     line,
     base,
     send1,
@@ -76,6 +86,16 @@
     hssem,
     hrsem,
 ):
+    sources = (
+        perm_in, state_in, pivot_in, offset_in, lower_in, upper_in, ajac_in, rjac_in, forcing_in
+    )
+    targets = (perm, state, pivot, offset, lower, upper, ajac, rjac, forcing)
+    loads = [
+        pltpu.make_async_copy(source, target, insem.at[i])
+        for i, (source, target) in enumerate(zip(sources, targets))
+    ]
+    for load in loads:
+        load.start()
     stations, radial = state.shape[1], state.shape[2]
     per = stations // count
     steps = radial // SEG
@@ -93,8 +113,10 @@
     for other in (up, down):
         pl.semaphore_signal(barrier, inc=1, device_id={"space": other}, device_id_type=MESH)
 
+    loads[0].wait()
     rows = lax.broadcasted_iota(jnp.int32, (radial, radial), 0)
     order = (rows == perm[...]).astype(f32).astype(jnp.bfloat16)
+    loads[1].wait()
     flat = select_columns(state[...].reshape(NV * stations, radial), order)
     for v in range(NV):
         block = flat[v * stations : (v + 1) * stations]
@@ -146,16 +168,16 @@
         q, crossed = w // 2, (v % 2) ^ (w % 2)
         return ((((kind * NP + p) * NP + q) * 2 + crossed) * 2 + h) * 8
 
-    tab[...] = jnp.zeros_like(tab)
+    for load in loads[2:]:
+        load.wait()
+    tab[864:, :] = jnp.zeros((32, radial), f32)
     for v in range(NV):
-        for k in range(8):
-            block = pivot[k, v]
-            for w in range(NV):
-                at = place(0, v, w) + k
-                tab[at : at + 1, :] = block[w : w + 1, :]
+        for w in range(NV):
+            at = place(0, v, w)
+            tab[at : at + 8, :] = pivot[v, w]
     for kind, matrix in ((1, lower), (2, upper)):
         for v in range(NV):
-            parts = [tab[place(0, v, u) : place(0, v, u) + 8, :] for u in range(NV)]
+            parts = [pivot[v, u] for u in range(NV)]
             for w in range(NV):
                 total = parts[0] * matrix[0, w]
                 for u in range(1, NV):
@@ -163,17 +185,20 @@
                 at = place(kind, v, w)
                 tab[at : at + 8, :] = -total
 
-    lane = lax.broadcasted_iota(jnp.int32, (128, 256), 1)
-    row = lax.broadcasted_iota(jnp.int32, (128, 256), 0)
-    wanted = offset[...]
+    lane = lax.broadcasted_iota(jnp.int32, (256, 256), 1)
+    row = lax.broadcasted_iota(jnp.int32, (256, 256), 0) % 128
+    wanted = jnp.concatenate([offset[...]] * 4, axis=1)
     for g in range(4):
         hit = (row - 32 * g == (lane // 64) * 8 + wanted)
         rhs[g] = hit.astype(f32).astype(jnp.bfloat16)
 
     def expand(b, carry):
         block = tab[pl.ds(pl.multiple_of(b * 128, 128), 128), :].T
+        high = block.astype(jnp.bfloat16)
+        low = (block - high.astype(f32)).astype(jnp.bfloat16)
+        pieces = jnp.concatenate([high, low], axis=1)
         for g in range(4):
-            both = select_columns(block, rhs[g])
+            both = jnp.dot(pieces, rhs[g], preferred_element_type=f32)
             coef[b * 8 + 2 * g] = both[:, :128]
             coef[b * 8 + 2 * g + 1] = both[:, 128:]
         return carry
@@ -205,6 +230,17 @@
             for p in range(NP)
         ]
 
+    for copy in first:
+        copy.wait_recv()
+    for n in range(count):
+        total = float(spectral[n, 0]) * recv1[0]
+        for m in range(1, count):
+            total = total + float(spectral[n, m]) * recv1[m]
+        send2[n] = total
+    second = exchange(send2, recv2, ssem2, rsem2)
+    for copy in second:
+        copy.start()
+    recv2[me] = send2[me]
     half = lax.broadcasted_iota(jnp.int32, (SEG, 128), 1) // 64
     unit = [
         [jnp.where(2 * q + half == u, 1.0, 0.0).astype(f32) for q in range(NP)] for u in range(NV)
@@ -222,7 +258,7 @@
                 new.append(got)
             return new
 
-        lax.fori_loop(0, steps, transfer, unit)
+        lax.fori_loop(0, steps, transfer, unit, unroll=2)
 
     order_forcing = select_columns(forcing[...].reshape(NV * stations, radial), order)
     for copy in halos:
@@ -259,17 +295,6 @@
     for v in range(NV):
         base[v] = base[v] - order_forcing[v * stations : (v + 1) * stations]
 
-    for copy in first:
-        copy.wait_recv()
-    for n in range(count):
-        total = float(spectral[n, 0]) * recv1[0]
-        for m in range(1, count):
-            total = total + float(spectral[n, m]) * recv1[m]
-        send2[n] = total
-    second = exchange(send2, recv2, ssem2, rsem2)
-    for copy in second:
-        copy.start()
-    recv2[me] = send2[me]
     for copy in second:
         copy.wait_recv()
 
@@ -311,7 +336,7 @@
             shift, edge = (1, 0) if kind == 0 else (SEG - 1, SEG - 1)
             return [jnp.where(segment == edge, 0.0, pltpu.roll(x, shift, 0)) for x in got]
 
-        return spread(lax.fori_loop(0, SEG - 1, turn, zeros))
+        return spread(lax.fori_loop(0, SEG - 1, turn, zeros, unroll=True))
 
     def forward(t, held):
         source = [sweep0[p, at_step(t), :] for p in range(NP)]
@@ -321,7 +346,7 @@
             sweep1[p, at_step(t), :] = got[p]
         return got
 
-    ends = lax.fori_loop(0, steps, forward, zeros)
+    ends = lax.fori_loop(0, steps, forward, zeros, unroll=4)
     entering = carries(0, steps - 1, ends)
 
     def backward(i, held):
@@ -332,7 +357,7 @@
             sweep0[p, at_step(t), :] = got[p]
         return got
 
-    ends = lax.fori_loop(0, steps, backward, zeros)
+    ends = lax.fori_loop(0, steps, backward, zeros, unroll=4)
     leaving = carries(1, 0, ends)
 
     def finish(t, carry):
@@ -341,7 +366,7 @@
             sweep1[p, at_step(t), :] = got[p]
         return carry
 
-    lax.fori_loop(0, steps, finish, 0)
+    lax.fori_loop(0, steps, finish, 0, unroll=4)
     for p in range(NP):
         block = sweep1[p].T
         cor_out[2 * p] = block[:stations]
@@ -368,15 +393,24 @@
     per = stations // count
     block = jax.ShapeDtypeStruct((variables, stations, radial), f32)
     vmem = pl.BlockSpec(memory_space=pltpu.VMEM)
-    smem = pl.BlockSpec(memory_space=pltpu.SMEM)
     dma = pltpu.SemaphoreType.DMA
     exchanged = pltpu.VMEM((count, variables * per, radial), f32)
     residual, correction = pl.pallas_call(
         functools.partial(kernel, count, spaces),
         out_shape=(block, block),
-        in_specs=[vmem] * 5 + [smem] * 4,
+        in_specs=[pl.BlockSpec(memory_space=pltpu.HBM)] * 9,
         out_specs=(vmem, vmem),
         scratch_shapes=[
+            pltpu.VMEM((variables, stations, radial), f32),
+            pltpu.VMEM((variables, stations, radial), f32),
+            pltpu.VMEM((variables, variables, 8, radial), f32),
+            pltpu.VMEM((1, stations), jnp.int32),
+            pltpu.VMEM((1, radial), jnp.int32),
+            pltpu.SMEM((variables, variables), f32),
+            pltpu.SMEM((variables, variables), f32),
+            pltpu.SMEM((variables, variables), f32),
+            pltpu.SMEM((variables, variables), f32),
+            dma((9,)),
             pltpu.VMEM((variables, stations + 16, radial), f32),
             pltpu.VMEM((variables, stations, radial), f32),
             exchanged,
@@ -388,7 +422,7 @@
             pltpu.VMEM((896, radial), f32),
             pltpu.VMEM((56, radial, 128), f32),
             pltpu.VMEM((36, radial, 128), f32),
-            pltpu.VMEM((4, 128, 256), jnp.bfloat16),
+            pltpu.VMEM((4, 256, 256), jnp.bfloat16),
             pltpu.VMEM((NP, radial, 128), f32),
             pltpu.VMEM((NP, radial, 128), f32),
             dma((count - 1,)),
@@ -399,13 +433,13 @@
             dma((2,)),
         ],
         compiler_params=pltpu.CompilerParams(
-            collective_id=0, has_side_effects=True, vmem_limit_bytes=40 * 1024 * 1024
+            collective_id=0, has_side_effects=True, vmem_limit_bytes=32 * 1024 * 1024
         ),
     )(
         flow_state[0],
         forcing[0],
-        pivot_table,
-        jnp.tile(block_offset, 4).reshape(1, 4 * stations),
+        jnp.transpose(pivot_table, (1, 2, 0, 3)),
+        block_offset.reshape(1, stations),
         line_perm.reshape(1, radial),
         axial_jac,
         radial_jac,

time: 29.8 us -> 28 us (0.940)
  Pallas kernels: 24.8 us -> 20.9 us
  local copies, waits for them, and re-layouts: 4.09 us -> 6.17 us
    pallas_call x1, Pallas kernels: 24.8 us -> 20.9 us  [shards(): pl.pallas_call(functools.partial(kernel, count, spaces), out_shape=(block...]
    unnamed x17 -> x20, local copies, waits for them, and re-layouts: 3.31 us -> 6.17 us
    another operation x2 -> x0, local copies, waits for them, and re-layouts: 0.78 us -> none  [shards(): jnp.tile(block_offset, 4).reshape(1, 4 * stations)]
where the time goes in v1:
time: 28 us; the launch traced here: 27.7 us
  Pallas kernels  20.9 us (75%)
  local copies, waits for them, and re-layouts  6.17 us (22%)
  between operations  0.68 us (2%)
    pallas_call x1, Pallas kernels, shards(): pl.pallas_call(functools.partial(kernel, count, spaces), out_shape=(block...  20.9 us
    unnamed x20, local copies, waits for them, and re-layouts  6.17 us

profile of v1, /device:TPU:0, one launch (start us, length us, event | category | flops | bytes accessed | tf_op | source)
XLA Modules:
  0.0 27.7 jit_solution(12710863322941190367)
XLA Ops:
  0.6 0.0 copy-start.4
  0.6 0.0 copy-start.3
  0.7 0.0 copy-start.7
  0.7 0.0 copy-start.8
  0.7 0.6 %copy-done.4 = f32[6,6]{1,0:T(8,128)S(1)} copy-done((f32[6,6]{1,0:T(8,128)S(1)}, f32[6,6]{1,0:T(8,128)}, u32[]{:S(2)}) %copy-start.4) | copy-done | bytes 168
  1.3 0.0 copy-done.3
  1.3 0.0 copy-done.7
  1.3 0.0 copy-done.8
  1.3 0.0 copy-start
  1.3 0.9 %copy-done = f32[1,6,64,128]{3,2,1,0:T(8,128)S(1)} copy-done((f32[1,6,64,128]{3,2,1,0:T(8,128)S(1)}, f32[1,6,64,128]{3,2,1,0:T(8,128)}, u32[]{:S(2)}) %copy-start) | copy-done | bytes 196632
  2.3 0.0 copy-start.1
  2.3 0.9 %copy-done.1 = f32[1,6,64,128]{3,2,1,0:T(8,128)S(1)} copy-done((f32[1,6,64,128]{3,2,1,0:T(8,128)S(1)}, f32[1,6,64,128]{3,2,1,0:T(8,128)}, u32[]{:S(2)}) %copy-start.1) | copy-done | bytes 196632
  3.2 0.0 copy-start.2
  3.2 0.9 %copy-done.2 = f32[8,6,6,128]{3,0,2,1:T(8,128)S(1)} copy-done((f32[8,6,6,128]{3,0,2,1:T(8,128)S(1)}, f32[8,6,6,128]{3,0,2,1:T(8,128)}, u32[]{:S(2)}) %copy-start.2) | copy-done | bytes 147480
  4.1 0.0 copy-start.5
  4.1 0.7 %copy-done.5 = f32[6,6]{1,0:T(8,128)S(1)} copy-done((f32[6,6]{1,0:T(8,128)S(1)}, f32[6,6]{1,0:T(8,128)}, u32[]{:S(2)}) %copy-start.5) | copy-done | bytes 168
  4.8 0.0 copy-start.6
  4.8 0.7 %copy-done.6 = f32[6,6]{1,0:T(8,128)S(1)} copy-done((f32[6,6]{1,0:T(8,128)S(1)}, f32[6,6]{1,0:T(8,128)}, u32[]{:S(2)}) %copy-start.6) | copy-done | bytes 168
  5.5 20.9 %shard_map.104 = (f32[6,64,128]{2,1,0:T(8,128)S(1)}, f32[6,64,128]{2,1,0:T(8,128)S(1)}) custom-call(f32[6,64,128]{2,1,0:T(8,128)S(1)} %bitcast.7, f32[6,64,128]{2,1,0:T(8,128)S(1)} %bitcast.8, f32[6,6,8,128]{3,2,1,0:T(8,128)S(1)} %bitcast.11, s32[1,64]{1,0:T(1,128)S(1)} %bitcast.12, s32[1,128]{1,0:T(1,128)S(1)} %bitcast.13, f32[6,6]{1,0:T(8,128)S(1)} %copy-done.3, ...), custom_call_target="tpu_custom_call" | custom-call | tf_op jit(solution)/shard_map/pallas_call | solution.py:398
  26.4 0.7 %copy.13 = f32[1,6,64,128]{3,2,1,0:T(8,128)} copy(f32[1,6,64,128]{3,2,1,0:T(8,128)S(1)} %bitcast.10) | data formatting | bytes 393216
  27.1 0.7 %copy.14 = f32[1,6,64,128]{3,2,1,0:T(8,128)} copy(f32[1,6,64,128]{3,2,1,0:T(8,128)S(1)} %bitcast.9) | data formatting | bytes 393216
Async XLA Ops:
  0.6 0.7 %copy-start.4 = (f32[6,6]{1,0:T(8,128)S(1)}, f32[6,6]{1,0:T(8,128)}, u32[]{:S(2)}) copy-start(f32[6,6]{1,0:T(8,128)} %rjac_in.1) | copy-start | bytes 436
  0.6 0.7 %copy-start.3 = (f32[6,6]{1,0:T(8,128)S(1)}, f32[6,6]{1,0:T(8,128)}, u32[]{:S(2)}) copy-start(f32[6,6]{1,0:T(8,128)} %ajac_in.1) | copy-start | bytes 436
  0.7 0.7 %copy-start.7 = (s32[64]{0:T(128)S(1)}, s32[64]{0:T(128)}, u32[]{:S(2)}) copy-start(s32[64]{0:T(128)} %param.12) | copy-start | bytes 772
  0.7 0.7 %copy-start.8 = (s32[128]{0:T(128)S(1)}, s32[128]{0:T(128)}, u32[]{:S(2)}) copy-start(s32[128]{0:T(128)} %param.13) | copy-start | bytes 1540
  1.3 0.9 %copy-start = (f32[1,6,64,128]{3,2,1,0:T(8,128)S(1)}, f32[1,6,64,128]{3,2,1,0:T(8,128)}, u32[]{:S(2)}) copy-start(f32[1,6,64,128]{3,2,1,0:T(8,128)} %param.9) | copy-start | bytes 589828
  2.3 0.9 %copy-start.1 = (f32[1,6,64,128]{3,2,1,0:T(8,128)S(1)}, f32[1,6,64,128]{3,2,1,0:T(8,128)}, u32[]{:S(2)}) copy-start(f32[1,6,64,128]{3,2,1,0:T(8,128)} %param.10) | copy-start | bytes 589828
  3.2 0.9 %copy-start.2 = (f32[8,6,6,128]{3,0,2,1:T(8,128)S(1)}, f32[8,6,6,128]{3,0,2,1:T(8,128)}, u32[]{:S(2)}) copy-start(f32[8,6,6,128]{3,0,2,1:T(8,128)} %param.11) | copy-start | bytes 442372
  4.1 0.7 %copy-start.5 = (f32[6,6]{1,0:T(8,128)S(1)}, f32[6,6]{1,0:T(8,128)}, u32[]{:S(2)}) copy-start(f32[6,6]{1,0:T(8,128)} %lower_in.1) | copy-start | bytes 436
  4.8 0.7 %copy-start.6 = (f32[6,6]{1,0:T(8,128)S(1)}, f32[6,6]{1,0:T(8,128)}, u32[]{:S(2)}) copy-start(f32[6,6]{1,0:T(8,128)} %upper_in.1) | copy-start | bytes 436

commit v2 on v1

--- a/solution.py
+++ b/solution.py
@@ -74,8 +74,10 @@
     halo_out,
     halo_in,
     tab,
-    coef,
+    pairc,
+    dupc,
     trans,
+    jump,
     rhs,
     sweep0,
     sweep1,
@@ -163,72 +165,62 @@
         copy.start()
     recv1[me] = send1[me]
 
-    def place(kind, v, w):
-        p, h = v // 2, v % 2
-        q, crossed = w // 2, (v % 2) ^ (w % 2)
-        return ((((kind * NP + p) * NP + q) * 2 + crossed) * 2 + h) * 8
-
     for load in loads[2:]:
         load.wait()
-    tab[864:, :] = jnp.zeros((32, radial), f32)
     for v in range(NV):
         for w in range(NV):
-            at = place(0, v, w)
+            at = (((v // 2 * NP + w // 2) * 2 + (v % 2 ^ w % 2)) * 2 + v % 2) * 8
             tab[at : at + 8, :] = pivot[v, w]
-    for kind, matrix in ((1, lower), (2, upper)):
+    tab[288:384, :] = jnp.zeros((96, radial), f32)
+    tab[960:, :] = jnp.zeros((64, radial), f32)
+    for kind, matrix in ((0, lower), (1, upper)):
         for v in range(NV):
             parts = [pivot[v, u] for u in range(NV)]
             for w in range(NV):
                 total = parts[0] * matrix[0, w]
                 for u in range(1, NV):
                     total = total + parts[u] * matrix[u, w]
-                at = place(kind, v, w)
+                at = 384 + ((kind * NV + v) * NV + w) * 8
                 tab[at : at + 8, :] = -total
 
     lane = lax.broadcasted_iota(jnp.int32, (256, 256), 1)
     row = lax.broadcasted_iota(jnp.int32, (256, 256), 0) % 128
     wanted = jnp.concatenate([offset[...]] * 4, axis=1)
     for g in range(4):
-        hit = (row - 32 * g == (lane // 64) * 8 + wanted)
+        hit = row - 32 * g == (lane // 64) * 8 + wanted
         rhs[g] = hit.astype(f32).astype(jnp.bfloat16)
-
-    def expand(b, carry):
-        block = tab[pl.ds(pl.multiple_of(b * 128, 128), 128), :].T
-        high = block.astype(jnp.bfloat16)
-        low = (block - high.astype(f32)).astype(jnp.bfloat16)
-        pieces = jnp.concatenate([high, low], axis=1)
-        for g in range(4):
-            both = jnp.dot(pieces, rhs[g], preferred_element_type=f32)
-            coef[b * 8 + 2 * g] = both[:, :128]
-            coef[b * 8 + 2 * g + 1] = both[:, 128:]
-        return carry
-
-    lax.fori_loop(0, tab.shape[0] // 128, expand, 0)
-
-    def at_step(t):
-        return pl.ds(t, SEG, stride=steps)
-
-    def crossed(pairs):
-        return [pltpu.roll(x, 64, 1) for x in pairs]
-
-    def apply(coefs, pairs, turned, start=None):
-        out = []
-        for p in range(NP):
-            total = None if start is None else start[p]
-            for q in range(NP):
-                term = coefs[p][q][0] * pairs[q] + coefs[p][q][1] * turned[q]
-                total = term if total is None else total + term
-            out.append(total)
-        return out
-
-    def load_coefs(kind, t):
-        return [
-            [
-                [coef[((kind * NP + p) * NP + q) * 2 + c, at_step(t), :] for c in range(2)]
-                for q in range(NP)
-            ]
-            for p in range(NP)
-        ]
+    for g in range(8):
+        hit = row - 16 * g == (lane // 128) * 8 + wanted
+        rhs[4 + g] = hit.astype(f32).astype(jnp.bfloat16)
+    target = lax.broadcasted_iota(jnp.int32, (radial, radial), 0)
+    origin = lax.broadcasted_iota(jnp.int32, (radial, radial), 1)
+    regroup = (origin == (target % SEG) * steps + target // SEG).astype(f32).astype(jnp.bfloat16)
+
+    def expand(first_block, first_rhs, groups, into):
+        def body(b, carry):
+            at = pl.multiple_of((first_block + b) * 128, 128)
+            block = tab[pl.ds(at, 128), :]
+            high = block.astype(jnp.bfloat16)
+            low = (block - high.astype(f32)).astype(jnp.bfloat16)
+            pieces = jnp.concatenate(
+                [
+                    lax.dot_general(
+                        regroup, x, (((1,), (1,)), ((), ())), preferred_element_type=f32
+                    ).astype(jnp.bfloat16)
+                    for x in (high, low)
+                ],
+                axis=1,
+            )
+            for g in range(groups):
+                both = jnp.dot(pieces, rhs[first_rhs + g], preferred_element_type=f32)
+                into[(b * groups + g) * 2] = both[:, :128]
+                into[(b * groups + g) * 2 + 1] = both[:, 128:]
+            return carry
+
+        return body
+
+    lax.fori_loop(0, 3, expand(0, 0, 4, pairc), 0)
+    lax.fori_loop(0, 5, expand(3, 4, 8, dupc), 0)
 
     for copy in first:
         copy.wait_recv()
@@ -241,7 +233,44 @@
     for copy in second:
         copy.start()
     recv2[me] = send2[me]
+    def at_step(t):
+        return pl.ds(t, SEG, stride=steps)
+
+    def rows_of(t):
+        return pl.ds(pl.multiple_of(t * SEG, SEG), SEG)
+
+    def crossed(pairs):
+        return [pltpu.roll(x, 64, 1) for x in pairs]
+
+    def add_up(terms):
+        while len(terms) > 1:
+            terms = [sum(terms[i : i + 2][1:], terms[i]) for i in range(0, len(terms), 2)]
+        return terms[0]
+
     half = lax.broadcasted_iota(jnp.int32, (SEG, 128), 1) // 64
+    segment = lax.broadcasted_iota(jnp.int32, (SEG, 128), 0)
+
+    def spread(pairs):
+        turned = crossed(pairs)
+        out = []
+        for q in range(NP):
+            out.append(jnp.where(half == 0, pairs[q], turned[q]))
+            out.append(jnp.where(half == 0, turned[q], pairs[q]))
+        return out
+
+    def paired(values):
+        return [jnp.where(half == 0, values[2 * p], values[2 * p + 1]) for p in range(NP)]
+
+    def load_dup(kind, t):
+        return [
+            [dupc[(kind * NV + v) * NV + w, rows_of(t), :] for w in range(NV)] for v in range(NV)
+        ]
+
+    def shifted(kind, values, by):
+        if kind == 0:
+            return [jnp.where(segment < by, 0.0, pltpu.roll(x, by, 0)) for x in values]
+        return [jnp.where(segment >= SEG - by, 0.0, pltpu.roll(x, SEG - by, 0)) for x in values]
+
     unit = [
         [jnp.where(2 * q + half == u, 1.0, 0.0).astype(f32) for q in range(NP)] for u in range(NV)
     ]
@@ -249,16 +278,48 @@
 
         def transfer(i, columns):
             t = i if kind == 0 else steps - 1 - i
-            coefs = load_coefs(kind + 1, t)
+            coefs = load_dup(kind, t)
+            straight = [
+                [
+                    jnp.where(half == 0, coefs[2 * p][2 * q], coefs[2 * p + 1][2 * q + 1])
+                    for q in range(NP)
+                ]
+                for p in range(NP)
+            ]
+            cross = [
+                [
+                    jnp.where(half == 0, coefs[2 * p][2 * q + 1], coefs[2 * p + 1][2 * q])
+                    for q in range(NP)
+                ]
+                for p in range(NP)
+            ]
             new = []
             for u in range(NV):
-                got = apply(coefs, columns[u], crossed(columns[u]))
+                turned = crossed(columns[u])
+                got = []
                 for p in range(NP):
-                    trans[(kind * NV + u) * NP + p, at_step(t), :] = got[p]
+                    terms = [straight[p][q] * columns[u][q] for q in range(NP)]
+                    terms += [cross[p][q] * turned[q] for q in range(NP)]
+                    got.append(add_up(terms))
+                    trans[(kind * NV + u) * NP + p, rows_of(t), :] = got[p]
                 new.append(got)
             return new
 
-        lax.fori_loop(0, steps, transfer, unit, unroll=2)
+        last = lax.fori_loop(0, steps, transfer, unit, unroll=2)
+        over = [shifted(kind, spread(last[u]), 1) for u in range(NV)]
+        for level in range(3):
+            for u in range(NV):
+                for v in range(NV):
+                    jump[((kind * 3 + level) * NV + v) * NV + u] = over[u][v]
+            if level < 2:
+                before = [shifted(kind, over[u], 1 << level) for u in range(NV)]
+                over = [
+                    [
+                        add_up([over[w][v] * before[u][w] for w in range(NV)])
+                        for v in range(NV)
+                    ]
+                    for u in range(NV)
+                ]
 
     order_forcing = select_columns(forcing[...].reshape(NV * stations, radial), order)
     for copy in halos:
@@ -310,58 +371,65 @@
             blocks.append(residual)
         sweep0[p] = jnp.concatenate(blocks, axis=0).T
 
-    zeros = [jnp.zeros((SEG, 128), f32) for _ in range(NP)]
-    segment = lax.broadcasted_iota(jnp.int32, (SEG, 128), 0)
-
-    def spread(pairs):
-        turned = crossed(pairs)
-        out = []
-        for q in range(NP):
-            out.append(jnp.where(half == 0, pairs[q], turned[q]))
-            out.append(jnp.where(half == 0, turned[q], pairs[q]))
-        return out
-
-    def add_transfer(kind, t, start, spreaded):
-        out = []
-        for p in range(NP):
-            total = start[p]
-            for u in range(NV):
-                total = total + trans[(kind * NV + u) * NP + p, at_step(t), :] * spreaded[u]
-            out.append(total)
-        return out
-
-    def carries(kind, last, ends):
-        def turn(i, held):
-            got = add_transfer(kind, last, ends, spread(held))
-            shift, edge = (1, 0) if kind == 0 else (SEG - 1, SEG - 1)
-            return [jnp.where(segment == edge, 0.0, pltpu.roll(x, shift, 0)) for x in got]
-
-        return spread(lax.fori_loop(0, SEG - 1, turn, zeros, unroll=True))
+    zeros = [jnp.zeros((SEG, 128), f32) for _ in range(NV)]
+
+    def add_transfer(kind, t, start, entering):
+        return [
+            add_up(
+                [start[p]]
+                + [
+                    trans[(kind * NV + u) * NP + p, rows_of(t), :] * entering[u]
+                    for u in range(NV)
+                ]
+            )
+            for p in range(NP)
+        ]
+
+    def advance(coefs, held, start):
+        return [
+            add_up([coefs[v][w] * held[w] for w in range(NV)]) + start[v] for v in range(NV)
+        ]
+
+    def carries(kind, ends):
+        held = shifted(kind, ends, 1)
+        for level in range(3):
+            base_at = (kind * 3 + level) * NV * NV
+            coefs = [[jump[base_at + v * NV + u] for u in range(NV)] for v in range(NV)]
+            held = advance(coefs, shifted(kind, held, 1 << level), held)
+        return held
 
     def forward(t, held):
         source = [sweep0[p, at_step(t), :] for p in range(NP)]
-        start = apply(load_coefs(0, t), source, crossed(source))
-        got = apply(load_coefs(1, t), held, crossed(held), start)
+        turned = crossed(source)
+        start = []
         for p in range(NP):
-            sweep1[p, at_step(t), :] = got[p]
+            terms = []
+            for q in range(NP):
+                at = (p * NP + q) * 2
+                terms.append(pairc[at, rows_of(t), :] * source[q])
+                terms.append(pairc[at + 1, rows_of(t), :] * turned[q])
+            start.append(add_up(terms))
+        got = advance(load_dup(0, t), held, spread(start))
+        for p, x in enumerate(paired(got)):
+            sweep1[p, rows_of(t), :] = x
         return got
 
-    ends = lax.fori_loop(0, steps, forward, zeros, unroll=4)
-    entering = carries(0, steps - 1, ends)
+    ends = lax.fori_loop(0, steps, forward, zeros, unroll=True)
+    entering = carries(0, ends)
 
     def backward(i, held):
         t = steps - 1 - i
-        start = add_transfer(0, t, [sweep1[p, at_step(t), :] for p in range(NP)], entering)
-        got = apply(load_coefs(2, t), held, crossed(held), start)
-        for p in range(NP):
-            sweep0[p, at_step(t), :] = got[p]
+        start = add_transfer(0, t, [sweep1[p, rows_of(t), :] for p in range(NP)], entering)
+        got = advance(load_dup(1, t), held, spread(start))
+        for p, x in enumerate(paired(got)):
+            sweep0[p, rows_of(t), :] = x
         return got
 
-    ends = lax.fori_loop(0, steps, backward, zeros, unroll=4)
-    leaving = carries(1, 0, ends)
+    ends = lax.fori_loop(0, steps, backward, zeros, unroll=True)
+    leaving = carries(1, ends)
 
     def finish(t, carry):
-        got = add_transfer(1, t, [sweep0[p, at_step(t), :] for p in range(NP)], leaving)
+        got = add_transfer(1, t, [sweep0[p, rows_of(t), :] for p in range(NP)], leaving)
         for p in range(NP):
             sweep1[p, at_step(t), :] = got[p]
         return carry
@@ -419,10 +487,12 @@
             exchanged,
             pltpu.VMEM((2, variables, radial), f32),
             pltpu.VMEM((2, variables, radial), f32),
-            pltpu.VMEM((896, radial), f32),
-            pltpu.VMEM((56, radial, 128), f32),
+            pltpu.VMEM((1024, radial), f32),
+            pltpu.VMEM((24, radial, 128), f32),
+            pltpu.VMEM((80, radial, 128), f32),
             pltpu.VMEM((36, radial, 128), f32),
-            pltpu.VMEM((4, 256, 256), jnp.bfloat16),
+            pltpu.VMEM((6 * variables * variables, SEG, 128), f32),
+            pltpu.VMEM((12, 256, 256), jnp.bfloat16),
             pltpu.VMEM((NP, radial, 128), f32),
             pltpu.VMEM((NP, radial, 128), f32),
             dma((count - 1,)),
@@ -436,15 +506,20 @@
             collective_id=0, has_side_effects=True, vmem_limit_bytes=32 * 1024 * 1024
         ),
     )(
-        flow_state[0],
-        forcing[0],
-        jnp.transpose(pivot_table, (1, 2, 0, 3)),
-        block_offset.reshape(1, stations),
-        line_perm.reshape(1, radial),
-        axial_jac,
-        radial_jac,
-        lower_block,
-        upper_block,
+        *(
+            pltpu.with_memory_space_constraint(x, pltpu.HBM)
+            for x in (
+                flow_state[0],
+                forcing[0],
+                jnp.transpose(pivot_table, (1, 2, 0, 3)),
+                block_offset.reshape(1, stations),
+                line_perm.reshape(1, radial),
+                axial_jac,
+                radial_jac,
+                lower_block,
+                upper_block,
+            )
+        )
     )
     return residual[None], correction[None]
 

time: 28 us -> 18.3 us (0.65)
  local copies, waits for them, and re-layouts: 6.17 us -> 1.36 us
  Pallas kernels: 20.9 us -> 16.1 us
    unnamed x20 -> x2, local copies, waits for them, and re-layouts: 6.17 us -> 1.36 us
    pallas_call x1, Pallas kernels: 20.9 us -> 16.1 us  [shards(): pl.pallas_call(functools.partial(kernel, count, spaces), out_shape=(block...]
where the time goes in v2:
time: 18.3 us; the launch traced here: 18.1 us
  Pallas kernels  16.1 us (88%)
  local copies, waits for them, and re-layouts  1.36 us (7%)
  between operations  0.64 us (3%)
    pallas_call x1, Pallas kernels, shards(): pl.pallas_call(functools.partial(kernel, count, spaces), out_shape=(block...  16.1 us
    unnamed x2, local copies, waits for them, and re-layouts  1.36 us

profile of v2, /device:TPU:0, one launch (start us, length us, event | category | flops | bytes accessed | tf_op | source)
XLA Modules:
  0.0 18.1 jit_solution(11366836746350485582)
XLA Ops:
  0.6 16.1 %shard_map.104 = (f32[6,64,128]{2,1,0:T(8,128)S(1)}, f32[6,64,128]{2,1,0:T(8,128)S(1)}) custom-call(f32[6,64,128]{2,1,0:T(8,128)} %bitcast.9, f32[6,64,128]{2,1,0:T(8,128)} %bitcast.10, f32[6,6,8,128]{3,2,1,0:T(8,128)} %bitcast.11, s32[1,64]{1,0:T(1,128)} %bitcast.12, s32[1,128]{1,0:T(1,128)} %bitcast.13, f32[6,6]{1,0:T(8,128)} %ajac_in.1, f32[6,6]{1,0:T(8,128)} %rjac_in.1, ...), custom_call_target="tpu_custom_call" | custom-call | tf_op jit(solution)/shard_map/pallas_call | solution.py:466
  16.8 0.7 %copy.13 = f32[1,6,64,128]{3,2,1,0:T(8,128)} copy(f32[1,6,64,128]{3,2,1,0:T(8,128)S(1)} %bitcast.8) | data formatting | bytes 393216
  17.4 0.7 %copy.14 = f32[1,6,64,128]{3,2,1,0:T(8,128)} copy(f32[1,6,64,128]{3,2,1,0:T(8,128)S(1)} %bitcast.7) | data formatting | bytes 393216

commit v3 on v2

--- a/solution.py
+++ b/solution.py
@@ -79,6 +79,7 @@
     trans,
     jump,
     rhs,
+    pieces,
     sweep0,
     sweep1,
     ssem1,
@@ -183,44 +184,51 @@
                 at = 384 + ((kind * NV + v) * NV + w) * 8
                 tab[at : at + 8, :] = -total
 
-    lane = lax.broadcasted_iota(jnp.int32, (256, 256), 1)
-    row = lax.broadcasted_iota(jnp.int32, (256, 256), 0) % 128
+    lane = lax.broadcasted_iota(jnp.int32, (32, 256), 1)
+    row = lax.broadcasted_iota(jnp.int32, (32, 256), 0)
     wanted = jnp.concatenate([offset[...]] * 4, axis=1)
+    rhs[...] = jnp.zeros_like(rhs)
+    hit = (row == (lane // 64) * 8 + wanted).astype(f32).astype(jnp.bfloat16)
     for g in range(4):
-        hit = row - 32 * g == (lane // 64) * 8 + wanted
-        rhs[g] = hit.astype(f32).astype(jnp.bfloat16)
+        for piece in (0, 128):
+            rhs[g, piece + 32 * g : piece + 32 * g + 32, :] = hit
+    hit = (row == (lane // 128) * 8 + wanted)[:16].astype(f32).astype(jnp.bfloat16)
     for g in range(8):
-        hit = row - 16 * g == (lane // 128) * 8 + wanted
-        rhs[4 + g] = hit.astype(f32).astype(jnp.bfloat16)
+        for piece in (0, 128):
+            rhs[4 + g, piece + 16 * g : piece + 16 * g + 16, :] = hit
     target = lax.broadcasted_iota(jnp.int32, (radial, radial), 0)
     origin = lax.broadcasted_iota(jnp.int32, (radial, radial), 1)
     regroup = (origin == (target % SEG) * steps + target // SEG).astype(f32).astype(jnp.bfloat16)
 
-    def expand(first_block, first_rhs, groups, into):
-        def body(b, carry):
-            at = pl.multiple_of((first_block + b) * 128, 128)
-            block = tab[pl.ds(at, 128), :]
-            high = block.astype(jnp.bfloat16)
-            low = (block - high.astype(f32)).astype(jnp.bfloat16)
-            pieces = jnp.concatenate(
-                [
-                    lax.dot_general(
-                        regroup, x, (((1,), (1,)), ((), ())), preferred_element_type=f32
-                    ).astype(jnp.bfloat16)
-                    for x in (high, low)
-                ],
-                axis=1,
+    def split(b, carry):
+        at = pl.multiple_of(b * 128, 128)
+        block = tab[pl.ds(at, 128), :]
+        high = block.astype(jnp.bfloat16)
+        low = (block - high.astype(f32)).astype(jnp.bfloat16)
+        for i, x in enumerate((high, low)):
+            pieces[pl.ds(at, 128), i * 128 : i * 128 + 128] = lax.dot_general(
+                regroup, x, (((1,), (1,)), ((), ())), preferred_element_type=f32
+            ).astype(jnp.bfloat16)
+        return carry
+
+    lax.fori_loop(0, 8, split, 0, unroll=2)
+
+    def expand(first_block, blocks, first_rhs, groups, into):
+        def body(g, carry):
+            both = jnp.dot(
+                pieces[first_block * 128 : (first_block + blocks) * 128, :],
+                rhs[first_rhs + g],
+                preferred_element_type=f32,
             )
-            for g in range(groups):
-                both = jnp.dot(pieces, rhs[first_rhs + g], preferred_element_type=f32)
-                into[(b * groups + g) * 2] = both[:, :128]
-                into[(b * groups + g) * 2 + 1] = both[:, 128:]
+            for b in range(blocks):
+                into[(b * groups + g) * 2] = both[b * 128 : b * 128 + 128, :128]
+                into[(b * groups + g) * 2 + 1] = both[b * 128 : b * 128 + 128, 128:]
             return carry
 
-        return body
-
-    lax.fori_loop(0, 3, expand(0, 0, 4, pairc), 0)
-    lax.fori_loop(0, 5, expand(3, 4, 8, dupc), 0)
+        lax.fori_loop(0, groups, body, 0)
+
+    expand(0, 3, 0, 4, pairc)
+    expand(3, 5, 4, 8, dupc)
 
     for copy in first:
         copy.wait_recv()
@@ -442,6 +450,17 @@
 
     for copy in first + halos + second:
         copy.wait_send()
+
+
+def deliver(residual, correction, res_out, cor_out, sem):
+    copies = [
+        pltpu.make_async_copy(residual, res_out, sem.at[0]),
+        pltpu.make_async_copy(correction, cor_out, sem.at[1]),
+    ]
+    for copy in copies:
+        copy.start()
+    for copy in copies:
+        copy.wait()
 
 
 def shards(
@@ -493,6 +512,7 @@
             pltpu.VMEM((36, radial, 128), f32),
             pltpu.VMEM((6 * variables * variables, SEG, 128), f32),
             pltpu.VMEM((12, 256, 256), jnp.bfloat16),
+            pltpu.VMEM((1024, 256), jnp.bfloat16),
             pltpu.VMEM((NP, radial, 128), f32),
             pltpu.VMEM((NP, radial, 128), f32),
             dma((count - 1,)),
@@ -521,6 +541,14 @@
             )
         )
     )
+    anywhere = pl.BlockSpec(memory_space=pl.ANY)
+    residual, correction = pl.pallas_call(
+        deliver,
+        out_shape=(block, block),
+        in_specs=[anywhere] * 2,
+        out_specs=(anywhere, anywhere),
+        scratch_shapes=[dma((2,))],
+    )(residual, correction)
     return residual[None], correction[None]
 
 

time: 18.3 us -> 31.3 us (1.71)
  Pallas kernels: 16.1 us -> 29.1 us
    pallas_call x0 -> x1, Pallas kernels: none -> 13 us  [shards(): pl.pallas_call(deliver, out_shape=(block, block), in_specs=[anywhere] * 2...]
    unnamed x2 -> x4, local copies, waits for them, and re-layouts: 1.36 us -> 1.35 us
where the time goes in v3:
time: 31.3 us; the launch traced here: 31.1 us
  Pallas kernels  29.1 us (93%)
  local copies, waits for them, and re-layouts  1.35 us (4%)
  between operations  0.65 us (2%)
    pallas_call x1, Pallas kernels, shards(): pl.pallas_call(functools.partial(kernel, count, spaces), out_shape=(block...  16.1 us
    pallas_call x1, Pallas kernels, shards(): pl.pallas_call(deliver, out_shape=(block, block), in_specs=[anywhere] * 2...  13 us
    unnamed x4, local copies, waits for them, and re-layouts  1.35 us

profile of v3, /device:TPU:0, one launch (start us, length us, event | category | flops | bytes accessed | tf_op | source)
XLA Modules:
  0.0 31.1 jit_solution(12393931509212129588)
XLA Ops:
  0.6 16.1 %shard_map.104 = (f32[6,64,128]{2,1,0:T(8,128)S(1)}, f32[6,64,128]{2,1,0:T(8,128)S(1)}) custom-call(f32[6,64,128]{2,1,0:T(8,128)} %bitcast.7, f32[6,64,128]{2,1,0:T(8,128)} %bitcast.8, f32[6,6,8,128]{3,2,1,0:T(8,128)} %bitcast.9, s32[1,64]{1,0:T(1,128)} %bitcast.10, s32[1,128]{1,0:T(1,128)} %bitcast.11, f32[6,6]{1,0:T(8,128)} %ajac_in.1, f32[6,6]{1,0:T(8,128)} %rjac_in.1, ...), custom_call_target="tpu_custom_call" | custom-call | tf_op jit(solution)/shard_map/pallas_call | solution.py:485
  16.8 0.0 copy-start
  16.8 0.7 %copy-done = f32[6,64,128]{2,1,0:T(8,128)} copy-done((f32[6,64,128]{2,1,0:T(8,128)}, f32[6,64,128]{2,1,0:T(8,128)S(1)}, u32[]{:S(2)}) %copy-start) | copy-done | bytes 196632
  17.4 0.0 copy-start.1
  17.4 0.7 %copy-done.1 = f32[6,64,128]{2,1,0:T(8,128)} copy-done((f32[6,64,128]{2,1,0:T(8,128)}, f32[6,64,128]{2,1,0:T(8,128)S(1)}, u32[]{:S(2)}) %copy-start.1) | copy-done | bytes 196632
  18.1 13.0 %shard_map.105 = (f32[6,64,128]{2,1,0:T(8,128)}, f32[6,64,128]{2,1,0:T(8,128)}) custom-call(f32[6,64,128]{2,1,0:T(8,128)} %copy-done, f32[6,64,128]{2,1,0:T(8,128)} %copy-done.1), custom_call_target="tpu_custom_call" | custom-call | tf_op jit(solution)/shard_map/pallas_call | solution.py:545
Async XLA Ops:
  16.8 0.7 %copy-start = (f32[6,64,128]{2,1,0:T(8,128)}, f32[6,64,128]{2,1,0:T(8,128)S(1)}, u32[]{:S(2)}) copy-start(f32[6,64,128]{2,1,0:T(8,128)S(1)} %get-tuple-element.6.residual) | copy-start | bytes 589828
  17.4 0.7 %copy-start.1 = (f32[6,64,128]{2,1,0:T(8,128)}, f32[6,64,128]{2,1,0:T(8,128)S(1)}, u32[]{:S(2)}) copy-start(f32[6,64,128]{2,1,0:T(8,128)S(1)} %get-tuple-element.7.correction) | copy-start | bytes 589828

commit v4 on v3

--- a/solution.py
+++ b/solution.py
@@ -88,6 +88,7 @@
     rsem2,
     hssem,
     hrsem,
+    go,
 ):
     sources = (
         perm_in, state_in, pivot_in, offset_in, lower_in, upper_in, ajac_in, rjac_in, forcing_in
@@ -109,12 +110,17 @@
     down = lax.rem(here + spaces - 1, spaces)
 
     barrier = pltpu.get_barrier_semaphore()
-    for d in range(1, count):
+    gate, informer = count - 1, count - 2
+    for n in range(gate):
+
+        @pl.when(me != n)
+        def _():
+            pl.semaphore_signal(barrier, inc=1, device_id={"inst": n}, device_id_type=MESH)
+
+    for other in (up, down):
         pl.semaphore_signal(
-            barrier, inc=1, device_id={"inst": lax.rem(me + d, count)}, device_id_type=MESH
+            barrier, inc=1, device_id={"inst": gate, "space": other}, device_id_type=MESH
         )
-    for other in (up, down):
-        pl.semaphore_signal(barrier, inc=1, device_id={"space": other}, device_id_type=MESH)
 
     loads[0].wait()
     rows = lax.broadcasted_iota(jnp.int32, (radial, radial), 0)
@@ -129,7 +135,17 @@
         for e in range(count):
             send1[e, v * per : (v + 1) * per, :] = block[e * per : (e + 1) * per]
 
-    pl.semaphore_wait(barrier, count + 1)
+    @pl.when(me != gate)
+    def _():
+        pl.semaphore_wait(barrier, count - 1)
+
+    @pl.when(me == informer)
+    def _():
+        pl.semaphore_signal(go, inc=1, device_id={"inst": gate}, device_id_type=MESH)
+
+    @pl.when(me == gate)
+    def _():
+        pl.semaphore_wait(go, 1)
 
     def exchange(source, target, ssem, rsem):
         copies = []
@@ -162,8 +178,6 @@
                 device_id_type=MESH,
             )
         )
-    for copy in halos:
-        copy.start()
     recv1[me] = send1[me]
 
     for load in loads[2:]:
@@ -230,6 +244,12 @@
     expand(0, 3, 0, 4, pairc)
     expand(3, 5, 4, 8, dupc)
 
+    @pl.when(me == gate)
+    def _():
+        pl.semaphore_wait(barrier, 2 * count)
+        for n in range(gate):
+            pl.semaphore_signal(go, inc=1, device_id={"inst": n}, device_id_type=MESH)
+
     for copy in first:
         copy.wait_recv()
     for n in range(count):
@@ -241,6 +261,14 @@
     for copy in second:
         copy.start()
     recv2[me] = send2[me]
+
+    @pl.when(me != gate)
+    def _():
+        pl.semaphore_wait(go, 1)
+
+    for copy in halos:
+        copy.start()
+
     def at_step(t):
         return pl.ds(t, SEG, stride=steps)
 
@@ -521,6 +549,7 @@
             dma((count - 1,)),
             dma((2,)),
             dma((2,)),
+            pltpu.SemaphoreType.REGULAR,
         ],
         compiler_params=pltpu.CompilerParams(
             collective_id=0, has_side_effects=True, vmem_limit_bytes=32 * 1024 * 1024
@@ -545,10 +574,13 @@
     residual, correction = pl.pallas_call(
         deliver,
         out_shape=(block, block),
-        in_specs=[anywhere] * 2,
+        in_specs=[vmem] * 2,
         out_specs=(anywhere, anywhere),
         scratch_shapes=[dma((2,))],
-    )(residual, correction)
+    )(
+        pltpu.with_memory_space_constraint(residual, pltpu.VMEM),
+        pltpu.with_memory_space_constraint(correction, pltpu.VMEM),
+    )
     return residual[None], correction[None]
 
 

time: 31.3 us -> 18.5 us (0.59)
  Pallas kernels: 29.1 us -> 17.7 us
  local copies, waits for them, and re-layouts: 1.35 us -> 0 us
    pallas_call x1, Pallas kernels: 13 us -> 0.76 us  [shards(): pl.pallas_call(deliver, out_shape=(block, block), in_specs=[vmem] * 2, ou...]
    unnamed x4 -> x0, local copies, waits for them, and re-layouts: 1.35 us -> none
    pallas_call x1, Pallas kernels: 16.1 us -> 16.9 us  [shards(): pl.pallas_call(functools.partial(kernel, count, spaces), out_shape=(block...]
where the time goes in v4:
time: 18.5 us; the launch traced here: 18.3 us
  Pallas kernels  17.7 us (96%)
  between operations  0.64 us (3%)
    pallas_call x1, Pallas kernels, shards(): pl.pallas_call(functools.partial(kernel, count, spaces), out_shape=(block...  16.9 us
    pallas_call x1, Pallas kernels, shards(): pl.pallas_call(deliver, out_shape=(block, block), in_specs=[vmem] * 2, ou...  0.76 us

profile of v4, /device:TPU:0, one launch (start us, length us, event | category | flops | bytes accessed | tf_op | source)
XLA Modules:
  0.0 18.3 jit_solution(14471849902421695733)
XLA Ops:
  0.6 16.9 %shard_map.104 = (f32[6,64,128]{2,1,0:T(8,128)S(1)}, f32[6,64,128]{2,1,0:T(8,128)S(1)}) custom-call(f32[6,64,128]{2,1,0:T(8,128)} %bitcast.7, f32[6,64,128]{2,1,0:T(8,128)} %bitcast.8, f32[6,6,8,128]{3,2,1,0:T(8,128)} %bitcast.9, s32[1,64]{1,0:T(1,128)} %bitcast.10, s32[1,128]{1,0:T(1,128)} %bitcast.11, f32[6,6]{1,0:T(8,128)} %ajac_in.1, f32[6,6]{1,0:T(8,128)} %rjac_in.1, ...), custom_call_target="tpu_custom_call" | custom-call | tf_op jit(solution)/shard_map/pallas_call | solution.py:513
  17.5 0.8 %shard_map.105 = (f32[6,64,128]{2,1,0:T(8,128)}, f32[6,64,128]{2,1,0:T(8,128)}) custom-call(f32[6,64,128]{2,1,0:T(8,128)S(1)} %get-tuple-element.6.residual, f32[6,64,128]{2,1,0:T(8,128)S(1)} %get-tuple-element.7.correction), custom_call_target="tpu_custom_call" | custom-call | tf_op jit(solution)/shard_map/pallas_call | solution.py:574

commit v5 on v4

--- a/solution.py
+++ b/solution.py
@@ -133,7 +133,8 @@
         halo_out[0, v : v + 1, :] = block[0:1]
         halo_out[1, v : v + 1, :] = block[stations - 1 : stations]
         for e in range(count):
-            send1[e, v * per : (v + 1) * per, :] = block[e * per : (e + 1) * per]
+            at = v % NP * per
+            send1[v // NP, e, at : at + per, :] = block[e * per : (e + 1) * per]
 
     @pl.when(me != gate)
     def _():
@@ -147,24 +148,24 @@
     def _():
         pl.semaphore_wait(go, 1)
 
-    def exchange(source, target, ssem, rsem):
+    def exchange(part, source, target, ssem, rsem):
         copies = []
         for d in range(count - 1, 0, -1):
             other = lax.rem(me + d, count)
             copies.append(
                 pltpu.make_async_remote_copy(
-                    src_ref=source.at[other],
-                    dst_ref=target.at[me],
-                    send_sem=ssem.at[d - 1],
-                    recv_sem=rsem.at[d - 1],
+                    src_ref=source.at[part, other],
+                    dst_ref=target.at[part, me],
+                    send_sem=ssem.at[part, d - 1],
+                    recv_sem=rsem.at[part, d - 1],
                     device_id={"inst": other},
                     device_id_type=MESH,
                 )
             )
         return copies
 
-    first = exchange(send1, recv1, ssem1, rsem1)
-    for copy in first:
+    first = [exchange(part, send1, recv1, ssem1, rsem1) for part in (0, 1)]
+    for copy in first[0] + first[1]:
         copy.start()
     halos = []
     for side, other in ((0, down), (1, up)):
@@ -178,7 +179,8 @@
                 device_id_type=MESH,
             )
         )
-    recv1[me] = send1[me]
+    for part in (0, 1):
+        recv1[part, me] = send1[part, me]
 
     for load in loads[2:]:
         load.wait()
@@ -227,6 +229,12 @@
 
     lax.fori_loop(0, 8, split, 0, unroll=2)
 
+    @pl.when(me == gate)
+    def _():
+        pl.semaphore_wait(barrier, 2 * count)
+        for n in range(gate):
+            pl.semaphore_signal(go, inc=1, device_id={"inst": n}, device_id_type=MESH)
+
     def expand(first_block, blocks, first_rhs, groups, into):
         def body(g, carry):
             both = jnp.dot(
@@ -244,30 +252,25 @@
     expand(0, 3, 0, 4, pairc)
     expand(3, 5, 4, 8, dupc)
 
-    @pl.when(me == gate)
-    def _():
-        pl.semaphore_wait(barrier, 2 * count)
-        for n in range(gate):
-            pl.semaphore_signal(go, inc=1, device_id={"inst": n}, device_id_type=MESH)
-
-    for copy in first:
-        copy.wait_recv()
-    for n in range(count):
-        total = float(spectral[n, 0]) * recv1[0]
-        for m in range(1, count):
-            total = total + float(spectral[n, m]) * recv1[m]
-        send2[n] = total
-    second = exchange(send2, recv2, ssem2, rsem2)
-    for copy in second:
-        copy.start()
-    recv2[me] = send2[me]
-
     @pl.when(me != gate)
     def _():
         pl.semaphore_wait(go, 1)
 
     for copy in halos:
         copy.start()
+
+    second = [exchange(part, send2, recv2, ssem2, rsem2) for part in (0, 1)]
+    for part in (0, 1):
+        for copy in first[part]:
+            copy.wait_recv()
+        for n in range(count):
+            total = float(spectral[n, 0]) * recv1[part, 0]
+            for m in range(1, count):
+                total = total + float(spectral[n, m]) * recv1[part, m]
+            send2[part, n] = total
+        for copy in second[part]:
+            copy.start()
+        recv2[part, me] = send2[part, me]
 
     def at_step(t):
         return pl.ds(t, SEG, stride=steps)
@@ -392,7 +395,7 @@
     for v in range(NV):
         base[v] = base[v] - order_forcing[v * stations : (v + 1) * stations]
 
-    for copy in second:
+    for copy in second[0] + second[1]:
         copy.wait_recv()
 
     pairs = []
@@ -400,7 +403,11 @@
         blocks = []
         for v in (2 * p, 2 * p + 1):
             timed = jnp.concatenate(
-                [recv2[e, v * per : (v + 1) * per, :] for e in range(count)], axis=0
+                [
+                    recv2[v // NP, e, v % NP * per : (v % NP + 1) * per, :]
+                    for e in range(count)
+                ],
+                axis=0,
             )
             residual = base[v] + timed
             res_out[v] = residual
@@ -476,7 +483,7 @@
         cor_out[2 * p] = block[:stations]
         cor_out[2 * p + 1] = block[stations:]
 
-    for copy in first + halos + second:
+    for copy in first[0] + first[1] + halos + second[0] + second[1]:
         copy.wait_send()
 
 
@@ -509,7 +516,7 @@
     block = jax.ShapeDtypeStruct((variables, stations, radial), f32)
     vmem = pl.BlockSpec(memory_space=pltpu.VMEM)
     dma = pltpu.SemaphoreType.DMA
-    exchanged = pltpu.VMEM((count, variables * per, radial), f32)
+    exchanged = pltpu.VMEM((2, count, NP * per, radial), f32)
     residual, correction = pl.pallas_call(
         functools.partial(kernel, count, spaces),
         out_shape=(block, block),
@@ -543,10 +550,10 @@
             pltpu.VMEM((1024, 256), jnp.bfloat16),
             pltpu.VMEM((NP, radial, 128), f32),
             pltpu.VMEM((NP, radial, 128), f32),
-            dma((count - 1,)),
-            dma((count - 1,)),
-            dma((count - 1,)),
-            dma((count - 1,)),
+            dma((2, count - 1)),
+            dma((2, count - 1)),
+            dma((2, count - 1)),
+            dma((2, count - 1)),
             dma((2,)),
             dma((2,)),
             pltpu.SemaphoreType.REGULAR,

time: 18.5 us -> 17.5 us (0.946)
  Pallas kernels: 17.7 us -> 16.7 us
    pallas_call x1, Pallas kernels: 16.9 us -> 15.9 us  [shards(): pl.pallas_call(functools.partial(kernel, count, spaces), out_shape=(block...]
where the time goes in v5:
time: 17.5 us; the launch traced here: 17.3 us
  Pallas kernels  16.7 us (95%)
  between operations  0.64 us (4%)
    pallas_call x1, Pallas kernels, shards(): pl.pallas_call(functools.partial(kernel, count, spaces), out_shape=(block...  15.9 us
    pallas_call x1, Pallas kernels, shards(): pl.pallas_call(deliver, out_shape=(block, block), in_specs=[vmem] * 2, ou...  0.76 us

profile of v5, /device:TPU:0, one launch (start us, length us, event | category | flops | bytes accessed | tf_op | source)
XLA Modules:
  0.0 17.3 jit_solution(6075362460428900820)
XLA Ops:
  0.6 15.9 %shard_map.104 = (f32[6,64,128]{2,1,0:T(8,128)S(1)}, f32[6,64,128]{2,1,0:T(8,128)S(1)}) custom-call(f32[6,64,128]{2,1,0:T(8,128)} %bitcast.7, f32[6,64,128]{2,1,0:T(8,128)} %bitcast.8, f32[6,6,8,128]{3,2,1,0:T(8,128)} %bitcast.9, s32[1,64]{1,0:T(1,128)} %bitcast.10, s32[1,128]{1,0:T(1,128)} %bitcast.11, f32[6,6]{1,0:T(8,128)} %ajac_in.1, f32[6,6]{1,0:T(8,128)} %rjac_in.1, ...), custom_call_target="tpu_custom_call" | custom-call | tf_op jit(solution)/shard_map/pallas_call | solution.py:520
  16.6 0.8 %shard_map.105 = (f32[6,64,128]{2,1,0:T(8,128)}, f32[6,64,128]{2,1,0:T(8,128)}) custom-call(f32[6,64,128]{2,1,0:T(8,128)S(1)} %get-tuple-element.6.residual, f32[6,64,128]{2,1,0:T(8,128)S(1)} %get-tuple-element.7.correction), custom_call_target="tpu_custom_call" | custom-call | tf_op jit(solution)/shard_map/pallas_call | solution.py:581

commit v6 on v5

--- a/solution.py
+++ b/solution.py
@@ -229,12 +229,6 @@
 
     lax.fori_loop(0, 8, split, 0, unroll=2)
 
-    @pl.when(me == gate)
-    def _():
-        pl.semaphore_wait(barrier, 2 * count)
-        for n in range(gate):
-            pl.semaphore_signal(go, inc=1, device_id={"inst": n}, device_id_type=MESH)
-
     def expand(first_block, blocks, first_rhs, groups, into):
         def body(g, carry):
             both = jnp.dot(
@@ -251,13 +245,6 @@
 
     expand(0, 3, 0, 4, pairc)
     expand(3, 5, 4, 8, dupc)
-
-    @pl.when(me != gate)
-    def _():
-        pl.semaphore_wait(go, 1)
-
-    for copy in halos:
-        copy.start()
 
     second = [exchange(part, send2, recv2, ssem2, rsem2) for part in (0, 1)]
     for part in (0, 1):
@@ -271,6 +258,20 @@
         for copy in second[part]:
             copy.start()
         recv2[part, me] = send2[part, me]
+        if part == 0:
+
+            @pl.when(me == gate)
+            def _():
+                pl.semaphore_wait(barrier, 2 * count)
+                for n in range(gate):
+                    pl.semaphore_signal(go, inc=1, device_id={"inst": n}, device_id_type=MESH)
+
+            @pl.when(me != gate)
+            def _():
+                pl.semaphore_wait(go, 1)
+
+            for copy in halos:
+                copy.start()
 
     def at_step(t):
         return pl.ds(t, SEG, stride=steps)
@@ -313,38 +314,42 @@
     unit = [
         [jnp.where(2 * q + half == u, 1.0, 0.0).astype(f32) for q in range(NP)] for u in range(NV)
     ]
+
+    def transfer_step(kind, i, columns):
+        t = i if kind == 0 else steps - 1 - i
+        coefs = load_dup(kind, t)
+        straight = [
+            [
+                jnp.where(half == 0, coefs[2 * p][2 * q], coefs[2 * p + 1][2 * q + 1])
+                for q in range(NP)
+            ]
+            for p in range(NP)
+        ]
+        cross = [
+            [
+                jnp.where(half == 0, coefs[2 * p][2 * q + 1], coefs[2 * p + 1][2 * q])
+                for q in range(NP)
+            ]
+            for p in range(NP)
+        ]
+        new = []
+        for u in range(NV):
+            turned = crossed(columns[u])
+            got = []
+            for p in range(NP):
+                terms = [straight[p][q] * columns[u][q] for q in range(NP)]
+                terms += [cross[p][q] * turned[q] for q in range(NP)]
+                got.append(add_up(terms))
+                trans[(kind * NV + u) * NP + p, rows_of(t), :] = got[p]
+            new.append(got)
+        return new
+
+    def transfer(i, both):
+        return [transfer_step(kind, i, both[kind]) for kind in (0, 1)]
+
+    lasts = lax.fori_loop(0, steps, transfer, [unit, unit])
     for kind in (0, 1):
-
-        def transfer(i, columns):
-            t = i if kind == 0 else steps - 1 - i
-            coefs = load_dup(kind, t)
-            straight = [
-                [
-                    jnp.where(half == 0, coefs[2 * p][2 * q], coefs[2 * p + 1][2 * q + 1])
-                    for q in range(NP)
-                ]
-                for p in range(NP)
-            ]
-            cross = [
-                [
-                    jnp.where(half == 0, coefs[2 * p][2 * q + 1], coefs[2 * p + 1][2 * q])
-                    for q in range(NP)
-                ]
-                for p in range(NP)
-            ]
-            new = []
-            for u in range(NV):
-                turned = crossed(columns[u])
-                got = []
-                for p in range(NP):
-                    terms = [straight[p][q] * columns[u][q] for q in range(NP)]
-                    terms += [cross[p][q] * turned[q] for q in range(NP)]
-                    got.append(add_up(terms))
-                    trans[(kind * NV + u) * NP + p, rows_of(t), :] = got[p]
-                new.append(got)
-            return new
-
-        last = lax.fori_loop(0, steps, transfer, unit, unroll=2)
+        last = lasts[kind]
         over = [shifted(kind, spread(last[u]), 1) for u in range(NV)]
         for level in range(3):
             for u in range(NV):

time: 17.5 us -> 18.8 us (1.074)
  Pallas kernels: 16.7 us -> 18 us
    pallas_call x1, Pallas kernels: 15.9 us -> 17.3 us  [shards(): pl.pallas_call(functools.partial(kernel, count, spaces), out_shape=(block...]
where the time goes in v6:
time: 18.8 us; the launch traced here: 18.7 us
  Pallas kernels  18 us (96%)
  between operations  0.64 us (3%)
    pallas_call x1, Pallas kernels, shards(): pl.pallas_call(functools.partial(kernel, count, spaces), out_shape=(block...  17.3 us
    pallas_call x1, Pallas kernels, shards(): pl.pallas_call(deliver, out_shape=(block, block), in_specs=[vmem] * 2, ou...  0.76 us

profile of v6, /device:TPU:0, one launch (start us, length us, event | category | flops | bytes accessed | tf_op | source)
XLA Modules:
  0.0 18.7 jit_solution(2536287553796034695)
XLA Ops:
  0.6 17.3 %shard_map.104 = (f32[6,64,128]{2,1,0:T(8,128)S(1)}, f32[6,64,128]{2,1,0:T(8,128)S(1)}) custom-call(f32[6,64,128]{2,1,0:T(8,128)} %bitcast.7, f32[6,64,128]{2,1,0:T(8,128)} %bitcast.8, f32[6,6,8,128]{3,2,1,0:T(8,128)} %bitcast.9, s32[1,64]{1,0:T(1,128)} %bitcast.10, s32[1,128]{1,0:T(1,128)} %bitcast.11, f32[6,6]{1,0:T(8,128)} %ajac_in.1, f32[6,6]{1,0:T(8,128)} %rjac_in.1, ...), custom_call_target="tpu_custom_call" | custom-call | tf_op jit(solution)/shard_map/pallas_call | solution.py:525
  17.9 0.8 %shard_map.105 = (f32[6,64,128]{2,1,0:T(8,128)}, f32[6,64,128]{2,1,0:T(8,128)}) custom-call(f32[6,64,128]{2,1,0:T(8,128)S(1)} %get-tuple-element.6.residual, f32[6,64,128]{2,1,0:T(8,128)S(1)} %get-tuple-element.7.correction), custom_call_target="tpu_custom_call" | custom-call | tf_op jit(solution)/shard_map/pallas_call | solution.py:586

commit v7 on v4

--- a/solution.py
+++ b/solution.py
@@ -250,6 +250,13 @@
         for n in range(gate):
             pl.semaphore_signal(go, inc=1, device_id={"inst": n}, device_id_type=MESH)
 
+    @pl.when(me != gate)
+    def _():
+        pl.semaphore_wait(go, 1)
+
+    for copy in halos:
+        copy.start()
+
     for copy in first:
         copy.wait_recv()
     for n in range(count):
@@ -261,13 +268,6 @@
     for copy in second:
         copy.start()
     recv2[me] = send2[me]
-
-    @pl.when(me != gate)
-    def _():
-        pl.semaphore_wait(go, 1)
-
-    for copy in halos:
-        copy.start()
 
     def at_step(t):
         return pl.ds(t, SEG, stride=steps)

time: 18.5 us -> 18.5 us (level)
  no operation moved by 1% of the time
where the time goes in v7:
time: 18.5 us; the launch traced here: 18.3 us
  Pallas kernels  17.7 us (96%)
  between operations  0.64 us (3%)
    pallas_call x1, Pallas kernels, shards(): pl.pallas_call(functools.partial(kernel, count, spaces), out_shape=(block...  16.9 us
    pallas_call x1, Pallas kernels, shards(): pl.pallas_call(deliver, out_shape=(block, block), in_specs=[vmem] * 2, ou...  0.76 us

profile of v7, /device:TPU:0, one launch (start us, length us, event | category | flops | bytes accessed | tf_op | source)
XLA Modules:
  0.0 18.3 jit_solution(8723622680080266603)
XLA Ops:
  0.6 16.9 %shard_map.104 = (f32[6,64,128]{2,1,0:T(8,128)S(1)}, f32[6,64,128]{2,1,0:T(8,128)S(1)}) custom-call(f32[6,64,128]{2,1,0:T(8,128)} %bitcast.7, f32[6,64,128]{2,1,0:T(8,128)} %bitcast.8, f32[6,6,8,128]{3,2,1,0:T(8,128)} %bitcast.9, s32[1,64]{1,0:T(1,128)} %bitcast.10, s32[1,128]{1,0:T(1,128)} %bitcast.11, f32[6,6]{1,0:T(8,128)} %ajac_in.1, f32[6,6]{1,0:T(8,128)} %rjac_in.1, ...), custom_call_target="tpu_custom_call" | custom-call | tf_op jit(solution)/shard_map/pallas_call | solution.py:513
  17.5 0.8 %shard_map.105 = (f32[6,64,128]{2,1,0:T(8,128)}, f32[6,64,128]{2,1,0:T(8,128)}) custom-call(f32[6,64,128]{2,1,0:T(8,128)S(1)} %get-tuple-element.6.residual, f32[6,64,128]{2,1,0:T(8,128)S(1)} %get-tuple-element.7.correction), custom_call_target="tpu_custom_call" | custom-call | tf_op jit(solution)/shard_map/pallas_call | solution.py:574
